TPU v7x, 32 devices: a whole 2x2x4 slice. The times are simulated.
32 devices in a mesh: gx: 4 (over y, x), gy: 8 (over z, core).
Axes of the slice: x: 2, y: 2, z: 4, core: 2. Of those that a mesh axis runs over, the one named last changes fastest.
Arguments:
- estimate: float32 [8, 512, 1024], P(None, 'gy', 'gx'), may hold values from 0.5 to 2
- views: float32 [4, 8, 512, 1024], P(None, None, 'gy', 'gx'), may hold values from 0.25 to 4
- psf_x: float32 [4, 15], replicated, may hold values from 0.05 to 1
- psf_y: float32 [4, 15], replicated, may hold values from 0.05 to 1
- psf_z: float32 [4, 15], replicated, may hold values from 0.05 to 1
- block_offsets: int32 [4, 2, 8, 4], replicated, may hold values from -15 to 15
- sub_shifts: int32 [4, 3, 8, 4], replicated, may hold values from 0 to 3
Outputs:
- estimate_next: float32 [8, 512, 1024], P(None, 'gy', 'gx')
All inputs are finite; a program needn't handle non-finite values.
Results may differ from a plain program's by a relative error of at most 0.0003.
Values sent between devices are 32-bit elements; how exact they have to be, the bound alone decides.
A program may use at most 64 MiB of HBM per device.

v0:
```python
import functools

import jax
import jax.numpy as jnp
from jax import lax
from jax.experimental import pallas as pl
from jax.experimental.pallas import tpu as pltpu
from jax.sharding import PartitionSpec as P

RADIUS = 7
HALO = 16
EDGE = 8
LANES = 128
MESH = pl.DeviceIdType.MESH
BF16 = jnp.bfloat16
F32 = jnp.float32

SIDES = [(dx, dy) for dx in (-1, 0, 1) for dy in (-1, 0, 1) if (dx, dy) != (0, 0)]
ROW_SIDES = [(0, -1), (0, 1)]
COL_SIDES = [side for side in SIDES if side[0] != 0]


def split(value):
    high = value.astype(BF16)
    return high, (value - high.astype(F32)).astype(BF16)


def dot3(a_high, a_low, b_high, b_low):
    total = jnp.dot(a_high, b_high, preferred_element_type=F32)
    total = total + jnp.dot(a_high, b_low, preferred_element_type=F32)
    return total + jnp.dot(a_low, b_high, preferred_element_type=F32)


def iota(shape, dim):
    return lax.broadcasted_iota(jnp.int32, shape, dim)


def taps_at(differ, taps):
    found = jnp.zeros(differ.shape, F32)
    for t, tap in enumerate(taps):
        found = jnp.where(differ == t, tap, found)
    return found


def group_of(lanes, width, count):
    group = jnp.zeros(lanes.shape, jnp.int32)
    for q in range(1, count):
        group = group + (lanes >= q * width).astype(jnp.int32)
    return group


def packed(tiles, first):
    lane = iota(tiles[0].shape, 1)
    result = jnp.zeros(tiles[0].shape, F32)
    for z, tile in enumerate(tiles):
        shift = (z * HALO - (0 if first else LANES - HALO)) % LANES
        moved = pltpu.roll(tile, shift, 1) if shift else tile
        result = jnp.where((lane >= z * HALO) & (lane < (z + 1) * HALO), moved, result)
    return result


def unpacked(strip, z, first):
    shift = ((0 if first else LANES - HALO) - z * HALO) % LANES
    return pltpu.roll(strip, shift, 1) if shift else strip


def kernel(
    sizes,
    est, views, psf_x, psf_y, psf_z, offs, subs, out,
    ext, own_first, own_last, from_left, from_right,
    e_high, e_low, bc_high, bc_low, bt_high, bt_low,
    f_high, f_low, g_high, g_low, blurred, ratio, acc,
    pack_right, pack_left, sum_left, sum_right, sum_rows,
    local_sem, est_send, est_recv, row_send, row_recv, col_send, col_recv, end_send, end_recv,
):
    count, planes, rows, cols = sizes
    wide = cols + LANES
    tall = rows + 2 * HALO
    mid = rows + 2 * EDGE
    taps_count = psf_x.shape[1]
    gx, gy = lax.axis_index("gx"), lax.axis_index("gy")
    nx, ny = lax.axis_size("gx"), lax.axis_size("gy")

    def exists(dx, dy):
        x, y = gx + dx, gy + dy
        return (x >= 0) & (x < nx) & (y >= 0) & (y < ny)

    def target(dx, dy):
        return {"gx": lax.rem(gx + dx + nx, nx), "gy": lax.rem(gy + dy + ny, ny)}

    def remote(src, dst, send, recv, side):
        return pltpu.make_async_remote_copy(
            src_ref=src, dst_ref=dst, send_sem=send, recv_sem=recv,
            device_id=target(*side), device_id_type=MESH,
        )

    def if_there(side, action):
        pl.when(exists(*side))(action)

    def take(copy, side, dst):
        if_there((-side[0], -side[1]), copy.wait_recv)

        @pl.when(jnp.logical_not(exists(-side[0], -side[1])))
        def _():
            dst[...] = jnp.zeros(dst.shape, F32)

    def rows_of(dy, depth):
        if dy == 0:
            return (0, rows), (HALO, rows)
        if dy == 1:
            return (rows - depth, depth), (HALO - depth, depth)
        return (0, depth), (HALO + rows, depth)

    loads = [
        pltpu.make_async_copy(views.at[v], ext.at[v, :, pl.ds(HALO, rows), pl.ds(0, cols)], local_sem.at[v])
        for v in range(count)
    ]
    loads.append(
        pltpu.make_async_copy(est, ext.at[count, :, pl.ds(HALO, rows), pl.ds(0, cols)], local_sem.at[count])
    )
    for load in loads[::-1]:
        load.start()
    barrier = pltpu.get_barrier_semaphore()
    for side in SIDES:
        if_there(
            side,
            lambda side=side: pl.semaphore_signal(
                barrier, inc=1, device_id=target(*side), device_id_type=MESH
            ),
        )

    def strips(v):
        own_first[v] = packed([ext[v, z, HALO : HALO + rows, 0:LANES] for z in range(planes)], True)
        own_last[v] = packed(
            [ext[v, z, HALO : HALO + rows, cols - LANES : cols] for z in range(planes)], False
        )

    loads[count].wait()
    strips(count)
    pl.semaphore_wait(barrier, sum(exists(*side).astype(jnp.int32) for side in SIDES))

    est_copies = []
    for i, side in enumerate(SIDES):
        dx, dy = side
        depth = EDGE if dx == 0 else HALO
        (src_at, src_rows), (dst_at, dst_rows) = rows_of(dy, depth)
        if dx == 0:
            src = est.at[:, pl.ds(src_at, src_rows), :]
            dst = ext.at[count, :, pl.ds(dst_at, dst_rows), pl.ds(0, cols)]
        else:
            own, land = (own_last, from_left) if dx == 1 else (own_first, from_right)
            src = own.at[count, pl.ds(src_at, src_rows), :]
            dst = land.at[count, pl.ds(dst_at, dst_rows), :]
        copy = remote(src, dst, est_send.at[i], est_recv.at[i], side)
        est_copies.append((copy, side, dst))
        if_there(side, copy.start)

    for load in loads[:count]:
        load.wait()
    lax.fori_loop(0, count, lambda v, c: (strips(v), c)[1], 0)
    col_copies = []
    for i, side in enumerate(COL_SIDES):
        dx, dy = side
        (src_at, src_rows), (dst_at, dst_rows) = rows_of(dy, HALO)
        own, land = (own_last, from_left) if dx == 1 else (own_first, from_right)
        src = own.at[pl.ds(0, count), pl.ds(src_at, src_rows), :]
        dst = land.at[pl.ds(0, count), pl.ds(dst_at, dst_rows), :]
        copy = remote(src, dst, col_send.at[i], col_recv.at[i], side)
        col_copies.append((copy, side, dst))
        if_there(side, copy.start)

    def row_copy(v, j):
        side = ROW_SIDES[j]
        (src_at, src_rows), (dst_at, dst_rows) = rows_of(side[1], HALO)
        src = views.at[v, :, pl.ds(src_at, src_rows), :]
        dst = ext.at[v, :, pl.ds(dst_at, dst_rows), pl.ds(0, cols)]
        return remote(src, dst, row_send.at[v, j], row_recv.at[v, j], side), side, dst

    for v in range(count):
        for j in range(2):
            copy, side, _ = row_copy(v, j)
            if_there(side, copy.start)

    for ref in (bc_high, bc_low, bt_high, bt_low):
        ref[...] = jnp.zeros(ref.shape, BF16)

    def build(v, carry):
        taps_x = [psf_x[v, t] for t in range(taps_count)]
        taps_y = [psf_y[v, t] for t in range(taps_count)]
        taps_z = [psf_z[v, t] for t in range(taps_count)]
        sum_x, sum_y, sum_z = sum(taps_x), sum(taps_y), sum(taps_z)
        piece = (LANES + 2 * HALO, LANES)
        differ = iota(piece, 0) - HALO - iota(piece, 1) + RADIUS
        scale = 1.0 / jnp.full((1, LANES), sum_x, F32)
        base = cols - LANES
        pieces = split(taps_at(differ, taps_x) * scale)
        for ref, part in zip((bc_high, bc_low), pieces):
            for c in range(0, cols, LANES):
                low = max(c - HALO, 0)
                high = c + LANES + HALO
                ref[v, low:high, c : c + LANES] = part[low - c + HALO : high - c + HALO]
            ref[v, wide - HALO : wide, 0:LANES] = part[0:HALO]
        pieces = split(taps_at(differ, taps_x[::-1]) * scale)
        for ref, part in zip((bt_high, bt_low), pieces):
            for c in range(0, cols, LANES):
                low = max(c - HALO, 0)
                high = min(c + LANES + HALO, cols)
                ref[v, low:high, c : c + LANES] = part[low - c + HALO : high - c + HALO]
            ref[v, cols - HALO : cols, cols:wide] = part[0:HALO]
            ref[v, 0:HALO, cols:wide] = part[LANES + HALO :]

        def both(shape, sign, lane_width):
            lane = iota((1, shape[1]), 1)
            group = group_of(lane, lane_width, planes)
            place = lane - group * lane_width
            if sign == 1:
                near = place - EDGE - iota(shape, 0) + RADIUS
            else:
                near = iota(shape, 0) - EDGE - place + RADIUS
            scale_zy = (1.0 / jnp.full((1, shape[1]), sum_y, F32)) * (
                1.0 / jnp.full((1, shape[1]), sum_z, F32)
            )
            row_band = taps_at(near, taps_y) * scale_zy
            deep = sign * (group - iota((planes, shape[1]), 0)) + RADIUS
            return row_band, taps_at(deep, taps_z)

        row_band, deep_band = both((rows, planes * mid), 1, mid)
        for z in range(planes):
            high, low = split(row_band * deep_band[z : z + 1])
            f_high[v, z * rows : (z + 1) * rows, :] = high
            f_low[v, z * rows : (z + 1) * rows, :] = low
        row_band, deep_band = both((mid, planes * rows), -1, rows)
        for z in range(planes):
            high, low = split(row_band * deep_band[z : z + 1])
            g_high[v, z * mid : (z + 1) * mid, :] = high
            g_low[v, z * mid : (z + 1) * mid, :] = low
        return carry

    lax.fori_loop(0, count, build, 0)

    def fill_side(v):
        for z in range(planes):
            right = unpacked(from_right[v], z, True)
            left = unpacked(from_left[v], z, False)
            lane = iota((tall, LANES), 1)
            value = jnp.where(lane < HALO, right, jnp.where(lane >= LANES - HALO, left, 0.0))
            ext[v, z, :, cols:wide] = value

    for copy, side, dst in est_copies:
        take(copy, side, dst)
    fill_side(count)
    for z in range(planes):
        high, low = split(ext[count, z, HALO - EDGE : HALO - EDGE + mid, :])
        e_high[z * mid : (z + 1) * mid, :] = high
        e_low[z * mid : (z + 1) * mid, :] = low

    def forward(v, carry):
        along = dot3(e_high[...], e_low[...], bc_high[v], bc_low[v])
        high, low = split(along)
        blurred[v] = dot3(f_high[v], f_low[v], high, low)
        return carry

    lax.fori_loop(0, count, forward, 0)

    for copy, side, dst in col_copies:
        take(copy, side, dst)
    acc[...] = jnp.zeros(acc.shape, F32)

    def one_view(v, carry):
        fill_side(v)
        for j in range(2):
            take(*row_copy(v, j))
        ox, oy = offs[v, 0, gy, gx], offs[v, 1, gy, gx]
        fx = subs[v, 0, gy, gx].astype(F32) * 0.25
        fy = subs[v, 1, gy, gx].astype(F32) * 0.25
        fz = subs[v, 2, gy, gx].astype(F32) * 0.25
        shift = jnp.where(ox > 0, LANES - ox, -ox)
        lane = iota((1, LANES), 1) + ox
        rest = oy + HALO
        for _ in range(2 * HALO // EDGE - 1):
            rest = jnp.where(rest >= EDGE, rest - EDGE, rest)
        turn = jnp.where(rest > 0, EDGE - rest, 0)
        within = iota((1, EDGE, LANES), 1) + rest < EDGE
        deep = rows + EDGE

        def plane(z):
            here = ext[v, z, 0:deep, :]
            for at in range(EDGE, 2 * HALO, EDGE):
                here = jnp.where(oy + HALO >= at, ext[v, z, at : at + deep, :], here)
            return (1.0 - fy) * here + fy * pltpu.roll(here, deep - 1, 0)

        below = None
        for z in range(planes - 1, -1, -1):
            here = plane(z)
            flat = (1.0 - fz) * here
            if below is not None:
                flat = flat + fz * below
            below = here
            flat = (1.0 - fx) * flat + fx * pltpu.roll(flat, wide - 1, 1)
            tiles = [
                pltpu.roll(flat[:, c : c + LANES], shift, 1) for c in range(0, wide, LANES)
            ]
            for i in range(cols // LANES):
                moved = jnp.where(
                    lane < 0, tiles[i - 1], jnp.where(lane < LANES, tiles[i], tiles[i + 1])
                )
                moved = pltpu.roll(moved.reshape(deep // EDGE, EDGE, LANES), turn, 1)
                moved = jnp.where(within, moved[:-1], moved[1:]).reshape(rows, LANES)
                at = pl.ds(z * rows, rows)
                part = pl.ds(i * LANES, LANES)
                ratio[at, part] = moved / blurred[v, at, part]
        high, low = split(ratio[...])
        spread = dot3(g_high[v], g_low[v], high, low)
        high, low = split(spread)
        acc[...] += dot3(high, low, bt_high[v], bt_low[v]).reshape(acc.shape)
        return carry

    lax.fori_loop(0, count, one_view, 0)

    side_tiles = [acc[z, :, cols:wide] for z in range(planes)]
    pack_right[...] = packed(side_tiles, True)
    pack_left[...] = packed(side_tiles, False)
    end_copies = []
    for i, side in enumerate(SIDES):
        dx, dy = side
        if dy == 0:
            src_at, dst_at, depth = EDGE, EDGE, rows
        elif dy == 1:
            src_at, dst_at, depth = EDGE + rows, 0, EDGE
        else:
            src_at, dst_at, depth = 0, EDGE + rows, EDGE
        if dx == 0:
            src = acc.at[:, pl.ds(src_at, EDGE), pl.ds(0, cols)]
            dst = sum_rows.at[(1 - dy) // 2]
        else:
            own, land = (pack_right, sum_left) if dx == 1 else (pack_left, sum_right)
            src = own.at[pl.ds(src_at, depth), :]
            dst = land.at[pl.ds(dst_at, depth), :]
        copy = remote(src, dst, end_send.at[i], end_recv.at[i], side)
        end_copies.append((copy, side, dst))
        if_there(side, copy.start)

    for copy, side, _ in est_copies + col_copies:
        if_there(side, copy.wait_send)
    for v in range(count):
        for j in range(2):
            copy, side, _ = row_copy(v, j)
            if_there(side, copy.wait_send)
    for copy, side, dst in end_copies:
        take(copy, side, dst)

    def folded(strip):
        blank = jnp.zeros((rows - EDGE, LANES), F32)
        main = strip[EDGE : EDGE + rows, :]
        main = main + jnp.concatenate([strip[0:EDGE, :], blank], axis=0)
        return main + jnp.concatenate([blank, strip[EDGE + rows :, :]], axis=0)

    left, right = folded(sum_left), folded(sum_right)
    lane = iota((rows, LANES), 1)
    weight = 1.0 / count
    for z in range(planes):
        for c in range(0, cols, LANES):
            total = acc[z, EDGE : EDGE + rows, c : c + LANES]
            if c == 0:
                total = total + jnp.where(lane < HALO, unpacked(left, z, True), 0.0)
            if c == cols - LANES:
                total = total + jnp.where(lane >= LANES - HALO, unpacked(right, z, False), 0.0)
            above = sum_rows[0, z, :, c : c + LANES]
            below = sum_rows[1, z, :, c : c + LANES]
            total = jnp.concatenate(
                [total[:EDGE] + above, total[EDGE : rows - EDGE], total[rows - EDGE :] + below], axis=0
            )
            own = ext[count, z, HALO : HALO + rows, c : c + LANES]
            out[z, :, c : c + LANES] = own * (total * weight)
    for copy, side, _ in end_copies:
        if_there(side, copy.wait_send)


def on_device(estimate, views, psf_x, psf_y, psf_z, block_offsets, sub_shifts):
    count, planes, rows, cols = views.shape
    wide, tall, mid = cols + LANES, rows + 2 * HALO, rows + 2 * EDGE
    vmem, dma = pltpu.VMEM, pltpu.SemaphoreType.DMA
    any_spec = pl.BlockSpec(memory_space=pl.ANY)
    smem = pl.BlockSpec(memory_space=pltpu.SMEM)
    return pl.pallas_call(
        functools.partial(kernel, (count, planes, rows, cols)),
        out_shape=jax.ShapeDtypeStruct(estimate.shape, F32),
        in_specs=[any_spec] * 2 + [smem] * 5,
        out_specs=pl.BlockSpec(memory_space=pltpu.VMEM),
        scratch_shapes=[
            vmem((count + 1, planes, tall, wide), F32),
            vmem((count + 1, rows, LANES), F32),
            vmem((count + 1, rows, LANES), F32),
            vmem((count + 1, tall, LANES), F32),
            vmem((count + 1, tall, LANES), F32),
            vmem((planes * mid, wide), BF16),
            vmem((planes * mid, wide), BF16),
            vmem((count, wide, cols), BF16),
            vmem((count, wide, cols), BF16),
            vmem((count, cols, wide), BF16),
            vmem((count, cols, wide), BF16),
            vmem((count, planes * rows, planes * mid), BF16),
            vmem((count, planes * rows, planes * mid), BF16),
            vmem((count, planes * mid, planes * rows), BF16),
            vmem((count, planes * mid, planes * rows), BF16),
            vmem((count, planes * rows, cols), F32),
            vmem((planes * rows, cols), F32),
            vmem((planes, mid, wide), F32),
            vmem((mid, LANES), F32),
            vmem((mid, LANES), F32),
            vmem((mid, LANES), F32),
            vmem((mid, LANES), F32),
            vmem((2, planes, EDGE, cols), F32),
            dma((count + 1,)),
            dma((len(SIDES),)),
            dma((len(SIDES),)),
            dma((count, 2)),
            dma((count, 2)),
            dma((len(COL_SIDES),)),
            dma((len(COL_SIDES),)),
            dma((len(SIDES),)),
            dma((len(SIDES),)),
        ],
        compiler_params=pltpu.CompilerParams(
            collective_id=0, has_side_effects=True, vmem_limit_bytes=48 * 1024 * 1024
        ),
    )(estimate, views, psf_x, psf_y, psf_z, block_offsets, sub_shifts)


def solution(mesh):
    in_specs = (P(None, "gy", "gx"), P(None, None, "gy", "gx"), P(), P(), P(), P(), P())
    out_specs = P(None, "gy", "gx")
    return jax.shard_map(
        on_device, mesh=mesh, in_specs=in_specs, out_specs=out_specs, check_vma=False
    )
```

profile of v0, /device:TPU:11, one launch (start us, length us, event | category | flops | bytes accessed | tf_op | source)
XLA Modules:
  0.0 43.5 jit_solution(9738711020714143019)
XLA Ops:
  0.0 0.8 %copy.8.offs = s32[4,2,8,4]{3,2,1,0:T(8,128)S(1)} copy(s32[4,2,8,4]{2,3,1,0:T(4,128)} %param.12) | data formatting | bytes 2048 | tf_op args[5]
  0.8 0.9 %copy.9.subs = s32[4,3,8,4]{3,2,1,0:T(8,128)S(1)} copy(s32[4,3,8,4]{2,3,1,0:T(4,128)} %param.13) | data formatting | bytes 3072 | tf_op args[6]
  1.7 0.0 copy-start
  1.7 1.6 %copy-done = f32[4,8,64,256]{3,2,1,0:T(8,128)S(1)} copy-done((f32[4,8,64,256]{3,2,1,0:T(8,128)S(1)}, f32[4,8,64,256]{3,2,1,0:T(8,128)}, u32[]{:S(2)}) %copy-start) | copy-done | bytes 2097176
  3.3 0.0 copy-start.1
  3.3 1.0 %copy-done.1 = f32[8,64,256]{2,1,0:T(8,128)S(1)} copy-done((f32[8,64,256]{2,1,0:T(8,128)S(1)}, f32[8,64,256]{2,1,0:T(8,128)}, u32[]{:S(2)}) %copy-start.1) | copy-done | bytes 524312
  4.3 0.0 copy-start.2
  4.3 0.7 %copy-done.2 = f32[4,15]{1,0:T(4,128)S(1)} copy-done((f32[4,15]{1,0:T(4,128)S(1)}, f32[4,15]{1,0:T(4,128)}, u32[]{:S(2)}) %copy-start.2) | copy-done | bytes 264
  5.0 0.0 copy-start.3
  5.0 0.7 %copy-done.3 = f32[4,15]{1,0:T(4,128)S(1)} copy-done((f32[4,15]{1,0:T(4,128)S(1)}, f32[4,15]{1,0:T(4,128)}, u32[]{:S(2)}) %copy-start.3) | copy-done | bytes 264
  5.7 0.0 copy-start.4
  5.7 0.7 %copy-done.4 = f32[4,15]{1,0:T(4,128)S(1)} copy-done((f32[4,15]{1,0:T(4,128)S(1)}, f32[4,15]{1,0:T(4,128)}, u32[]{:S(2)}) %copy-start.4) | copy-done | bytes 264
  6.4 36.3 %shard_map.73 = f32[8,64,256]{2,1,0:T(8,128)S(1)} custom-call(f32[8,64,256]{2,1,0:T(8,128)S(1)} %copy-done.1, f32[4,8,64,256]{3,2,1,0:T(8,128)S(1)} %copy-done, f32[4,15]{1,0:T(4,128)S(1)} %copy-done.2, f32[4,15]{1,0:T(4,128)S(1)} %copy-done.3, f32[4,15]{1,0:T(4,128)S(1)} %copy-done.4, s32[4,2,8,4]{3,2,1,0:T(8,128)S(1)} %copy.8.offs, ...), custom_call_target="tpu_custom_call" | custom-call | tf_op jit(solution)/shard_map/pallas_call | solution.py:385
  42.7 0.8 %copy.11 = f32[8,64,256]{2,1,0:T(8,128)} copy(f32[8,64,256]{2,1,0:T(8,128)S(1)} %shard_map.73) | data formatting | bytes 1048576
Async XLA Ops:
  1.7 1.6 %copy-start = (f32[4,8,64,256]{3,2,1,0:T(8,128)S(1)}, f32[4,8,64,256]{3,2,1,0:T(8,128)}, u32[]{:S(2)}) copy-start(f32[4,8,64,256]{3,2,1,0:T(8,128)} %views.1) | copy-start | bytes 6291460
  3.3 1.0 %copy-start.1 = (f32[8,64,256]{2,1,0:T(8,128)S(1)}, f32[8,64,256]{2,1,0:T(8,128)}, u32[]{:S(2)}) copy-start(f32[8,64,256]{2,1,0:T(8,128)} %est.1) | copy-start | bytes 1572868
  4.3 0.7 %copy-start.2 = (f32[4,15]{1,0:T(4,128)S(1)}, f32[4,15]{1,0:T(4,128)}, u32[]{:S(2)}) copy-start(f32[4,15]{1,0:T(4,128)} %psf_x.1) | copy-start | bytes 724
  5.0 0.7 %copy-start.3 = (f32[4,15]{1,0:T(4,128)S(1)}, f32[4,15]{1,0:T(4,128)}, u32[]{:S(2)}) copy-start(f32[4,15]{1,0:T(4,128)} %psf_y.1) | copy-start | bytes 724
  5.7 0.7 %copy-start.4 = (f32[4,15]{1,0:T(4,128)S(1)}, f32[4,15]{1,0:T(4,128)}, u32[]{:S(2)}) copy-start(f32[4,15]{1,0:T(4,128)} %psf_z.1) | copy-start | bytes 724
where the time goes:
time: 43.9 us; the launch traced here: 43.5 us
  Pallas kernels  36.3 us (83%)
  local copies, waits for them, and re-layouts  7.18 us (16%)
    pallas_call x1, Pallas kernels, on_device(): pl.pallas_call(functools.partial(kernel, (count, planes, rows, cols)), ou...  36.3 us
    unnamed x13, local copies, waits for them, and re-layouts  7.18 us

commit v1 on v0

--- a/solution.py
+++ b/solution.py
@@ -25,10 +25,8 @@
     return high, (value - high.astype(F32)).astype(BF16)
 
 
-def dot3(a_high, a_low, b_high, b_low):
-    total = jnp.dot(a_high, b_high, preferred_element_type=F32)
-    total = total + jnp.dot(a_high, b_low, preferred_element_type=F32)
-    return total + jnp.dot(a_low, b_high, preferred_element_type=F32)
+def dot(a, b):
+    return jnp.dot(a, b, preferred_element_type=F32)
 
 
 def iota(shape, dim):
@@ -66,12 +64,12 @@
 
 def kernel(
     sizes,
-    est, views, psf_x, psf_y, psf_z, offs, subs, out,
+    est, views, psf_x_in, psf_y_in, psf_z_in, offs_in, subs_in, out,
+    psf_x, psf_y, psf_z, offs, subs,
     ext, own_first, own_last, from_left, from_right,
-    e_high, e_low, bc_high, bc_low, bt_high, bt_low,
-    f_high, f_low, g_high, g_low, blurred, ratio, acc,
+    e_high, e_low, bands_c, bands_t, bands_f, bands_g, blurred, ratio, acc,
     pack_right, pack_left, sum_left, sum_right, sum_rows,
-    local_sem, est_send, est_recv, row_send, row_recv, col_send, col_recv, end_send, end_recv,
+    local_sem, small_sem, est_send, est_recv, row_send, row_recv, col_send, col_recv, end_send, end_recv,
 ):
     count, planes, rows, cols = sizes
     wide = cols + LANES
@@ -119,6 +117,14 @@
         pltpu.make_async_copy(est, ext.at[count, :, pl.ds(HALO, rows), pl.ds(0, cols)], local_sem.at[count])
     )
     for load in loads[::-1]:
+        load.start()
+    small = [
+        pltpu.make_async_copy(src, dst, small_sem.at[i])
+        for i, (src, dst) in enumerate(
+            ((psf_x_in, psf_x), (psf_y_in, psf_y), (psf_z_in, psf_z), (offs_in, offs), (subs_in, subs))
+        )
+    ]
+    for load in small:
         load.start()
     barrier = pltpu.get_barrier_semaphore()
     for side in SIDES:
@@ -181,59 +187,68 @@
             copy, side, _ = row_copy(v, j)
             if_there(side, copy.start)
 
-    for ref in (bc_high, bc_low, bt_high, bt_low):
-        ref[...] = jnp.zeros(ref.shape, BF16)
+    for load in small:
+        load.wait()
+    bands_c[...] = jnp.zeros(bands_c.shape, BF16)
+    bands_t[...] = jnp.zeros(bands_t.shape, BF16)
 
     def build(v, carry):
         taps_x = [psf_x[v, t] for t in range(taps_count)]
         taps_y = [psf_y[v, t] for t in range(taps_count)]
         taps_z = [psf_z[v, t] for t in range(taps_count)]
-        sum_x, sum_y, sum_z = sum(taps_x), sum(taps_y), sum(taps_z)
+
+        def inverse(taps, lanes):
+            return 1.0 / jnp.full((1, lanes), sum(taps), F32)
+
         piece = (LANES + 2 * HALO, LANES)
         differ = iota(piece, 0) - HALO - iota(piece, 1) + RADIUS
-        scale = 1.0 / jnp.full((1, LANES), sum_x, F32)
-        base = cols - LANES
-        pieces = split(taps_at(differ, taps_x) * scale)
-        for ref, part in zip((bc_high, bc_low), pieces):
-            for c in range(0, cols, LANES):
-                low = max(c - HALO, 0)
-                high = c + LANES + HALO
-                ref[v, low:high, c : c + LANES] = part[low - c + HALO : high - c + HALO]
-            ref[v, wide - HALO : wide, 0:LANES] = part[0:HALO]
-        pieces = split(taps_at(differ, taps_x[::-1]) * scale)
-        for ref, part in zip((bt_high, bt_low), pieces):
-            for c in range(0, cols, LANES):
-                low = max(c - HALO, 0)
-                high = min(c + LANES + HALO, cols)
-                ref[v, low:high, c : c + LANES] = part[low - c + HALO : high - c + HALO]
-            ref[v, cols - HALO : cols, cols:wide] = part[0:HALO]
-            ref[v, 0:HALO, cols:wide] = part[LANES + HALO :]
-
-        def both(shape, sign, lane_width):
-            lane = iota((1, shape[1]), 1)
-            group = group_of(lane, lane_width, planes)
-            place = lane - group * lane_width
-            if sign == 1:
-                near = place - EDGE - iota(shape, 0) + RADIUS
-            else:
-                near = iota(shape, 0) - EDGE - place + RADIUS
-            scale_zy = (1.0 / jnp.full((1, shape[1]), sum_y, F32)) * (
-                1.0 / jnp.full((1, shape[1]), sum_z, F32)
-            )
-            row_band = taps_at(near, taps_y) * scale_zy
-            deep = sign * (group - iota((planes, shape[1]), 0)) + RADIUS
-            return row_band, taps_at(deep, taps_z)
-
-        row_band, deep_band = both((rows, planes * mid), 1, mid)
+        scale = inverse(taps_x, LANES)
+        part = (taps_at(differ, taps_x) * scale).astype(BF16)
+        for c in range(0, cols, LANES):
+            low = max(c - HALO, 0)
+            high = c + LANES + HALO
+            bands_c[v, low:high, c : c + LANES] = part[low - c + HALO : high - c + HALO]
+        bands_c[v, wide - HALO : wide, 0:LANES] = part[0:HALO]
+        part = (taps_at(differ, taps_x[::-1]) * scale).astype(BF16)
+        for c in range(0, cols, LANES):
+            low = max(c - HALO, 0)
+            high = min(c + LANES + HALO, cols)
+            bands_t[v, low:high, c : c + LANES] = part[low - c + HALO : high - c + HALO]
+        bands_t[v, cols - HALO : cols, cols:wide] = part[0:HALO]
+        bands_t[v, 0:HALO, cols:wide] = part[LANES + HALO :]
+
+        def deep_band(width, lanes, sign):
+            group = group_of(iota((planes, lanes), 1), width, planes)
+            band = taps_at(sign * (group - iota((planes, lanes), 0)) + RADIUS, taps_z)
+            return band * inverse(taps_z, lanes)
+
+        def tiled(band, lanes):
+            return jnp.concatenate([band] * (lanes // band.shape[1]), axis=1)
+
+        scale = inverse(taps_y, LANES)
+        block = planes * rows
+        lane = iota((1, LANES), 1)
+        place = lane - group_of(lane, rows, LANES // rows) * rows
+        near = taps_at(place - iota((rows, LANES), 0) + RADIUS, taps_y) * scale
+        deep = deep_band(rows, block, 1)
+        near = tiled(near, block)
         for z in range(planes):
-            high, low = split(row_band * deep_band[z : z + 1])
-            f_high[v, z * rows : (z + 1) * rows, :] = high
-            f_low[v, z * rows : (z + 1) * rows, :] = low
-        row_band, deep_band = both((mid, planes * rows), -1, rows)
+            bands_f[v, z * rows : (z + 1) * rows, 0:block] = (near * deep[z : z + 1]).astype(BF16)
+        beside = planes * HALO
+        lane = iota((1, beside), 1)
+        place = lane - group_of(lane, HALO, planes) * HALO
+        place = jnp.where(place < EDGE, place - EDGE, place + (rows - EDGE))
+        near = taps_at(place - iota((rows, beside), 0) + RADIUS, taps_y) * scale[:, 0:1]
+        deep = deep_band(HALO, beside, 1)
         for z in range(planes):
-            high, low = split(row_band * deep_band[z : z + 1])
-            g_high[v, z * mid : (z + 1) * mid, :] = high
-            g_low[v, z * mid : (z + 1) * mid, :] = low
+            bands_f[v, z * rows : (z + 1) * rows, block:] = (near * deep[z : z + 1]).astype(BF16)
+        lane = iota((1, LANES), 1)
+        place = lane - group_of(lane, rows, LANES // rows) * rows
+        near = taps_at(iota((mid, LANES), 0) - EDGE - place + RADIUS, taps_y) * scale
+        deep = deep_band(rows, block, -1)
+        near = tiled(near, block)
+        for z in range(planes):
+            bands_g[v, z * mid : (z + 1) * mid, :] = (near * deep[z : z + 1]).astype(BF16)
         return carry
 
     lax.fori_loop(0, count, build, 0)
@@ -249,15 +264,23 @@
     for copy, side, dst in est_copies:
         take(copy, side, dst)
     fill_side(count)
+    block = planes * rows
     for z in range(planes):
-        high, low = split(ext[count, z, HALO - EDGE : HALO - EDGE + mid, :])
-        e_high[z * mid : (z + 1) * mid, :] = high
-        e_low[z * mid : (z + 1) * mid, :] = low
+        high, low = split(ext[count, z, HALO : HALO + rows, :])
+        e_high[z * rows : (z + 1) * rows, :] = high
+        e_low[z * rows : (z + 1) * rows, :] = low
+        beside = jnp.concatenate(
+            [ext[count, z, HALO - EDGE : HALO, :], ext[count, z, HALO + rows : HALO + rows + EDGE, :]],
+            axis=0,
+        )
+        high, low = split(beside)
+        e_high[block + z * HALO : block + (z + 1) * HALO, :] = high
+        e_low[block + z * HALO : block + (z + 1) * HALO, :] = low
 
     def forward(v, carry):
-        along = dot3(e_high[...], e_low[...], bc_high[v], bc_low[v])
+        along = dot(e_high[...], bands_c[v]) + dot(e_low[...], bands_c[v])
         high, low = split(along)
-        blurred[v] = dot3(f_high[v], f_low[v], high, low)
+        blurred[v] = dot(bands_f[v], high) + dot(bands_f[v], low)
         return carry
 
     lax.fori_loop(0, count, forward, 0)
@@ -270,10 +293,10 @@
         fill_side(v)
         for j in range(2):
             take(*row_copy(v, j))
-        ox, oy = offs[v, 0, gy, gx], offs[v, 1, gy, gx]
-        fx = subs[v, 0, gy, gx].astype(F32) * 0.25
-        fy = subs[v, 1, gy, gx].astype(F32) * 0.25
-        fz = subs[v, 2, gy, gx].astype(F32) * 0.25
+        ox, oy = offs[v, 0, gx, gy], offs[v, 1, gx, gy]
+        fx = subs[v, 0, gx, gy].astype(F32) * 0.25
+        fy = subs[v, 1, gx, gy].astype(F32) * 0.25
+        fz = subs[v, 2, gx, gy].astype(F32) * 0.25
         shift = jnp.where(ox > 0, LANES - ox, -ox)
         lane = iota((1, LANES), 1) + ox
         rest = oy + HALO
@@ -287,7 +310,7 @@
             here = ext[v, z, 0:deep, :]
             for at in range(EDGE, 2 * HALO, EDGE):
                 here = jnp.where(oy + HALO >= at, ext[v, z, at : at + deep, :], here)
-            return (1.0 - fy) * here + fy * pltpu.roll(here, deep - 1, 0)
+            return here
 
         below = None
         for z in range(planes - 1, -1, -1):
@@ -304,15 +327,17 @@
                 moved = jnp.where(
                     lane < 0, tiles[i - 1], jnp.where(lane < LANES, tiles[i], tiles[i + 1])
                 )
+                moved = (1.0 - fy) * moved + fy * pltpu.roll(moved, deep - 1, 0)
                 moved = pltpu.roll(moved.reshape(deep // EDGE, EDGE, LANES), turn, 1)
                 moved = jnp.where(within, moved[:-1], moved[1:]).reshape(rows, LANES)
                 at = pl.ds(z * rows, rows)
                 part = pl.ds(i * LANES, LANES)
                 ratio[at, part] = moved / blurred[v, at, part]
         high, low = split(ratio[...])
-        spread = dot3(g_high[v], g_low[v], high, low)
+        spread = dot(bands_g[v], high) + dot(bands_g[v], low)
         high, low = split(spread)
-        acc[...] += dot3(high, low, bt_high[v], bt_low[v]).reshape(acc.shape)
+        total = dot(high, bands_t[v]) + dot(low, bands_t[v])
+        acc[...] += total.reshape(acc.shape)
         return carry
 
     lax.fori_loop(0, count, one_view, 0)
@@ -381,13 +406,19 @@
     wide, tall, mid = cols + LANES, rows + 2 * HALO, rows + 2 * EDGE
     vmem, dma = pltpu.VMEM, pltpu.SemaphoreType.DMA
     any_spec = pl.BlockSpec(memory_space=pl.ANY)
-    smem = pl.BlockSpec(memory_space=pltpu.SMEM)
+    offsets = block_offsets.transpose(0, 1, 3, 2)
+    shifts = sub_shifts.transpose(0, 1, 3, 2)
     return pl.pallas_call(
         functools.partial(kernel, (count, planes, rows, cols)),
         out_shape=jax.ShapeDtypeStruct(estimate.shape, F32),
-        in_specs=[any_spec] * 2 + [smem] * 5,
+        in_specs=[any_spec] * 7,
         out_specs=pl.BlockSpec(memory_space=pltpu.VMEM),
         scratch_shapes=[
+            pltpu.SMEM(psf_x.shape, F32),
+            pltpu.SMEM(psf_y.shape, F32),
+            pltpu.SMEM(psf_z.shape, F32),
+            pltpu.SMEM(offsets.shape, jnp.int32),
+            pltpu.SMEM(shifts.shape, jnp.int32),
             vmem((count + 1, planes, tall, wide), F32),
             vmem((count + 1, rows, LANES), F32),
             vmem((count + 1, rows, LANES), F32),
@@ -396,12 +427,8 @@
             vmem((planes * mid, wide), BF16),
             vmem((planes * mid, wide), BF16),
             vmem((count, wide, cols), BF16),
-            vmem((count, wide, cols), BF16),
-            vmem((count, cols, wide), BF16),
             vmem((count, cols, wide), BF16),
             vmem((count, planes * rows, planes * mid), BF16),
-            vmem((count, planes * rows, planes * mid), BF16),
-            vmem((count, planes * mid, planes * rows), BF16),
             vmem((count, planes * mid, planes * rows), BF16),
             vmem((count, planes * rows, cols), F32),
             vmem((planes * rows, cols), F32),
@@ -412,6 +439,7 @@
             vmem((mid, LANES), F32),
             vmem((2, planes, EDGE, cols), F32),
             dma((count + 1,)),
+            dma((5,)),
             dma((len(SIDES),)),
             dma((len(SIDES),)),
             dma((count, 2)),
@@ -422,9 +450,9 @@
             dma((len(SIDES),)),
         ],
         compiler_params=pltpu.CompilerParams(
-            collective_id=0, has_side_effects=True, vmem_limit_bytes=48 * 1024 * 1024
+            collective_id=0, has_side_effects=True, vmem_limit_bytes=62 * 1024 * 1024
         ),
-    )(estimate, views, psf_x, psf_y, psf_z, block_offsets, sub_shifts)
+    )(estimate, views, psf_x, psf_y, psf_z, offsets, shifts)
 
 
 def solution(mesh):

time: 43.9 us -> 31.1 us (0.71)
  Pallas kernels: 36.3 us -> 29 us
  local copies, waits for them, and re-layouts: 7.18 us -> 1.87 us
    pallas_call x1, Pallas kernels: 36.3 us -> 29 us  [on_device(): pl.pallas_call(functools.partial(kernel, (count, planes, rows, cols)), ou...]
    unnamed x13 -> x1, local copies, waits for them, and re-layouts: 7.18 us -> 1.87 us
where the time goes in v1:
time: 31.1 us; the launch traced here: 30.9 us
  Pallas kernels  29 us (93%)
  local copies, waits for them, and re-layouts  1.87 us (6%)
    pallas_call x1, Pallas kernels, on_device(): pl.pallas_call(functools.partial(kernel, (count, planes, rows, cols)), ou...  29 us
    unnamed x1, local copies, waits for them, and re-layouts  1.87 us

profile of v1, /device:TPU:11, one launch (start us, length us, event | category | flops | bytes accessed | tf_op | source)
XLA Modules:
  0.0 30.9 jit_solution(8639443217608544492)
XLA Ops:
  0.0 29.0 %shard_map.73 = f32[8,64,256]{2,1,0:T(8,128)} custom-call(f32[8,64,256]{2,1,0:T(8,128)} %est.1, f32[4,8,64,256]{3,2,1,0:T(8,128)} %views.1, f32[4,15]{1,0:T(4,128)} %psf_x_in.1, f32[4,15]{1,0:T(4,128)} %psf_y_in.1, f32[4,15]{1,0:T(4,128)} %psf_z_in.1, s32[4,2,4,8]{3,2,1,0:T(4,128)} %bitcast.3, s32[4,3,4,8]{3,2,1,0:T(4,128)} %bitcast.2), custom_call_target="tpu_custom_call" | custom-call | tf_op jit(solution)/shard_map/pallas_call | solution.py:411
  29.0 1.9 %copy.9 = f32[8,64,256]{2,1,0:T(8,128)} copy(f32[8,64,256]{2,1,0:T(8,128)} %shard_map.73) | data formatting | bytes 1048576

commit v2 on v1

--- a/solution.py
+++ b/solution.py
@@ -67,7 +67,8 @@
     est, views, psf_x_in, psf_y_in, psf_z_in, offs_in, subs_in, out,
     psf_x, psf_y, psf_z, offs, subs,
     ext, own_first, own_last, from_left, from_right,
-    e_high, e_low, bands_c, bands_t, bands_f, bands_g, blurred, ratio, acc,
+    e_high, e_low, bands_c, bands_t, bands_f, bands_g, blurred, ratio,
+    spread_high, spread_low, acc, acc_rows,
     pack_right, pack_left, sum_left, sum_right, sum_rows,
     local_sem, small_sem, est_send, est_recv, row_send, row_recv, col_send, col_recv, end_send, end_recv,
 ):
@@ -161,6 +162,18 @@
         est_copies.append((copy, side, dst))
         if_there(side, copy.start)
 
+    def row_copy(v, j):
+        side = ROW_SIDES[j]
+        (src_at, src_rows), (dst_at, dst_rows) = rows_of(side[1], HALO)
+        src = views.at[v, :, pl.ds(src_at, src_rows), :]
+        dst = ext.at[v, :, pl.ds(dst_at, dst_rows), pl.ds(0, cols)]
+        return remote(src, dst, row_send.at[v, j], row_recv.at[v, j], side), side, dst
+
+    for v in range(count):
+        for j in range(2):
+            copy, side, _ = row_copy(v, j)
+            if_there(side, copy.start)
+
     for load in loads[:count]:
         load.wait()
     lax.fori_loop(0, count, lambda v, c: (strips(v), c)[1], 0)
@@ -174,18 +187,6 @@
         copy = remote(src, dst, col_send.at[i], col_recv.at[i], side)
         col_copies.append((copy, side, dst))
         if_there(side, copy.start)
-
-    def row_copy(v, j):
-        side = ROW_SIDES[j]
-        (src_at, src_rows), (dst_at, dst_rows) = rows_of(side[1], HALO)
-        src = views.at[v, :, pl.ds(src_at, src_rows), :]
-        dst = ext.at[v, :, pl.ds(dst_at, dst_rows), pl.ds(0, cols)]
-        return remote(src, dst, row_send.at[v, j], row_recv.at[v, j], side), side, dst
-
-    for v in range(count):
-        for j in range(2):
-            copy, side, _ = row_copy(v, j)
-            if_there(side, copy.start)
 
     for load in small:
         load.wait()
@@ -246,9 +247,13 @@
         place = lane - group_of(lane, rows, LANES // rows) * rows
         near = taps_at(iota((mid, LANES), 0) - EDGE - place + RADIUS, taps_y) * scale
         deep = deep_band(rows, block, -1)
-        near = tiled(near, block)
+        beside = tiled(jnp.concatenate([near[:EDGE], near[EDGE + rows :]], axis=0), block)
+        near = tiled(near[EDGE : EDGE + rows], block)
         for z in range(planes):
-            bands_g[v, z * mid : (z + 1) * mid, :] = (near * deep[z : z + 1]).astype(BF16)
+            band = (near * deep[z : z + 1]).astype(BF16)
+            bands_g[v, z * rows : (z + 1) * rows, :] = band
+            band = (beside * deep[z : z + 1]).astype(BF16)
+            bands_g[v, block + z * HALO : block + (z + 1) * HALO, :] = band
         return carry
 
     lax.fori_loop(0, count, build, 0)
@@ -277,22 +282,22 @@
         e_high[block + z * HALO : block + (z + 1) * HALO, :] = high
         e_low[block + z * HALO : block + (z + 1) * HALO, :] = low
 
-    def forward(v, carry):
+    def forward(v):
         along = dot(e_high[...], bands_c[v]) + dot(e_low[...], bands_c[v])
         high, low = split(along)
         blurred[v] = dot(bands_f[v], high) + dot(bands_f[v], low)
-        return carry
-
-    lax.fori_loop(0, count, forward, 0)
+
+    for v in range(count):
+        forward(v)
 
     for copy, side, dst in col_copies:
         take(copy, side, dst)
-    acc[...] = jnp.zeros(acc.shape, F32)
-
-    def one_view(v, carry):
-        fill_side(v)
+    for v in range(count):
         for j in range(2):
             take(*row_copy(v, j))
+
+    def one_view(v):
+        fill_side(v)
         ox, oy = offs[v, 0, gx, gy], offs[v, 1, gx, gy]
         fx = subs[v, 0, gx, gy].astype(F32) * 0.25
         fy = subs[v, 1, gx, gy].astype(F32) * 0.25
@@ -332,19 +337,30 @@
                 moved = jnp.where(within, moved[:-1], moved[1:]).reshape(rows, LANES)
                 at = pl.ds(z * rows, rows)
                 part = pl.ds(i * LANES, LANES)
-                ratio[at, part] = moved / blurred[v, at, part]
-        high, low = split(ratio[...])
+                ratio[v, at, part] = moved / blurred[v, at, part]
+        high, low = split(ratio[v])
         spread = dot(bands_g[v], high) + dot(bands_g[v], low)
         high, low = split(spread)
-        total = dot(high, bands_t[v]) + dot(low, bands_t[v])
-        acc[...] += total.reshape(acc.shape)
-        return carry
-
-    lax.fori_loop(0, count, one_view, 0)
-
-    side_tiles = [acc[z, :, cols:wide] for z in range(planes)]
-    pack_right[...] = packed(side_tiles, True)
-    pack_left[...] = packed(side_tiles, False)
+        at = pl.ds(v * cols, cols)
+        spread_high[:, at] = high
+        spread_low[:, at] = low
+
+    for v in range(count):
+        one_view(v)
+
+    def along_cols(first, last, low, high):
+        band = bands_t[:, :, low:high].reshape(count * cols, high - low)
+        return dot(spread_high[first:last, :], band) + dot(spread_low[first:last, :], band)
+
+    border = along_cols(block, block + planes * HALO, 0, wide)
+    border = border.reshape(planes, HALO, wide)
+    acc_rows[...] = border[:, :, :cols]
+    beside = along_cols(0, block, cols, wide).reshape(planes, rows, LANES)
+    for pack, first in ((pack_right, True), (pack_left, False)):
+        pack[EDGE : EDGE + rows, :] = packed([beside[z] for z in range(planes)], first)
+        ends = packed([border[z, :, cols:] for z in range(planes)], first)
+        pack[0:EDGE, :] = ends[:EDGE]
+        pack[EDGE + rows :, :] = ends[EDGE:]
     end_copies = []
     for i, side in enumerate(SIDES):
         dx, dy = side
@@ -355,7 +371,7 @@
         else:
             src_at, dst_at, depth = 0, EDGE + rows, EDGE
         if dx == 0:
-            src = acc.at[:, pl.ds(src_at, EDGE), pl.ds(0, cols)]
+            src = acc_rows.at[:, pl.ds(0 if dy == -1 else EDGE, EDGE), :]
             dst = sum_rows.at[(1 - dy) // 2]
         else:
             own, land = (pack_right, sum_left) if dx == 1 else (pack_left, sum_right)
@@ -365,6 +381,8 @@
         end_copies.append((copy, side, dst))
         if_there(side, copy.start)
 
+    acc[...] = along_cols(0, block, 0, cols)
+
     for copy, side, _ in est_copies + col_copies:
         if_there(side, copy.wait_send)
     for v in range(count):
@@ -385,7 +403,7 @@
     weight = 1.0 / count
     for z in range(planes):
         for c in range(0, cols, LANES):
-            total = acc[z, EDGE : EDGE + rows, c : c + LANES]
+            total = acc[z * rows : (z + 1) * rows, c : c + LANES]
             if c == 0:
                 total = total + jnp.where(lane < HALO, unpacked(left, z, True), 0.0)
             if c == cols - LANES:
@@ -395,8 +413,7 @@
             total = jnp.concatenate(
                 [total[:EDGE] + above, total[EDGE : rows - EDGE], total[rows - EDGE :] + below], axis=0
             )
-            own = ext[count, z, HALO : HALO + rows, c : c + LANES]
-            out[z, :, c : c + LANES] = own * (total * weight)
+            out[z, :, c : c + LANES] = total * weight
     for copy, side, _ in end_copies:
         if_there(side, copy.wait_send)
 
@@ -408,7 +425,7 @@
     any_spec = pl.BlockSpec(memory_space=pl.ANY)
     offsets = block_offsets.transpose(0, 1, 3, 2)
     shifts = sub_shifts.transpose(0, 1, 3, 2)
-    return pl.pallas_call(
+    mean_back = pl.pallas_call(
         functools.partial(kernel, (count, planes, rows, cols)),
         out_shape=jax.ShapeDtypeStruct(estimate.shape, F32),
         in_specs=[any_spec] * 7,
@@ -431,8 +448,11 @@
             vmem((count, planes * rows, planes * mid), BF16),
             vmem((count, planes * mid, planes * rows), BF16),
             vmem((count, planes * rows, cols), F32),
+            vmem((count, planes * rows, cols), F32),
+            vmem((planes * mid, count * cols), BF16),
+            vmem((planes * mid, count * cols), BF16),
             vmem((planes * rows, cols), F32),
-            vmem((planes, mid, wide), F32),
+            vmem((planes, HALO, cols), F32),
             vmem((mid, LANES), F32),
             vmem((mid, LANES), F32),
             vmem((mid, LANES), F32),
@@ -453,6 +473,7 @@
             collective_id=0, has_side_effects=True, vmem_limit_bytes=62 * 1024 * 1024
         ),
     )(estimate, views, psf_x, psf_y, psf_z, offsets, shifts)
+    return estimate * mean_back
 
 
 def solution(mesh):

time: 31.1 us -> 27.2 us (0.87)
  Pallas kernels: 29 us -> 25.1 us
  other arithmetic: 0 us -> 1.9 us
  local copies, waits for them, and re-layouts: 1.87 us -> 0.01 us
    pallas_call x1, Pallas kernels: 29 us -> 25.1 us  [on_device(): pl.pallas_call(functools.partial(kernel, (count, planes, rows, cols)), ou...]
    mul x0 -> x1, other arithmetic: none -> 1.9 us  [on_device(): return estimate * mean_back]
    unnamed x1 -> x2, local copies, waits for them, and re-layouts: 1.87 us -> 0.01 us
where the time goes in v2:
time: 27.2 us; the launch traced here: 27 us
  Pallas kernels  25.1 us (92%)
  other arithmetic  1.9 us (7%)
    pallas_call x1, Pallas kernels, on_device(): pl.pallas_call(functools.partial(kernel, (count, planes, rows, cols)), ou...  25.1 us
    mul x1, other arithmetic, on_device(): return estimate * mean_back  1.9 us

profile of v2, /device:TPU:11, one launch (start us, length us, event | category | flops | bytes accessed | tf_op | source)
XLA Modules:
  0.0 27.0 jit_solution(16498254762646537883)
XLA Ops:
  0.0 0.0 copy-start
  0.0 25.1 %shard_map.73 = f32[8,64,256]{2,1,0:T(8,128)} custom-call(f32[8,64,256]{2,1,0:T(8,128)} %est.1, f32[4,8,64,256]{3,2,1,0:T(8,128)} %views.1, f32[4,15]{1,0:T(4,128)} %psf_x_in.1, f32[4,15]{1,0:T(4,128)} %psf_y_in.1, f32[4,15]{1,0:T(4,128)} %psf_z_in.1, s32[4,2,4,8]{3,2,1,0:T(4,128)} %bitcast.3, s32[4,3,4,8]{3,2,1,0:T(4,128)} %bitcast.2), custom_call_target="tpu_custom_call" | custom-call | tf_op jit(solution)/shard_map/pallas_call | solution.py:428
  25.1 0.0 copy-done
  25.1 1.9 %mul.3 = f32[8,64,256]{2,1,0:T(8,128)} multiply(f32[8,64,256]{2,1,0:T(8,128)S(1)} %copy-done, f32[8,64,256]{2,1,0:T(8,128)} %shard_map.73) | non-fusion elementwise | flops 131072 | bytes 1572864 | tf_op jit(solution)/shard_map/mul | solution.py:476
Async XLA Ops:
  0.0 25.1 %copy-start = (f32[8,64,256]{2,1,0:T(8,128)S(1)}, f32[8,64,256]{2,1,0:T(8,128)}, u32[]{:S(2)}) copy-start(f32[8,64,256]{2,1,0:T(8,128)} %est.1) | copy-start | bytes 1572868

commit v3 on v2

--- a/solution.py
+++ b/solution.py
@@ -193,14 +193,11 @@
     bands_c[...] = jnp.zeros(bands_c.shape, BF16)
     bands_t[...] = jnp.zeros(bands_t.shape, BF16)
 
-    def build(v, carry):
+    def inverse(taps, lanes):
+        return 1.0 / jnp.full((1, lanes), sum(taps), F32)
+
+    def build_cols(v, carry):
         taps_x = [psf_x[v, t] for t in range(taps_count)]
-        taps_y = [psf_y[v, t] for t in range(taps_count)]
-        taps_z = [psf_z[v, t] for t in range(taps_count)]
-
-        def inverse(taps, lanes):
-            return 1.0 / jnp.full((1, lanes), sum(taps), F32)
-
         piece = (LANES + 2 * HALO, LANES)
         differ = iota(piece, 0) - HALO - iota(piece, 1) + RADIUS
         scale = inverse(taps_x, LANES)
@@ -217,6 +214,13 @@
             bands_t[v, low:high, c : c + LANES] = part[low - c + HALO : high - c + HALO]
         bands_t[v, cols - HALO : cols, cols:wide] = part[0:HALO]
         bands_t[v, 0:HALO, cols:wide] = part[LANES + HALO :]
+        return carry
+
+    lax.fori_loop(0, count, build_cols, 0)
+
+    def build_rows(v):
+        taps_y = [psf_y[v, t] for t in range(taps_count)]
+        taps_z = [psf_z[v, t] for t in range(taps_count)]
 
         def deep_band(width, lanes, sign):
             group = group_of(iota((planes, lanes), 1), width, planes)
@@ -254,9 +258,6 @@
             bands_g[v, z * rows : (z + 1) * rows, :] = band
             band = (beside * deep[z : z + 1]).astype(BF16)
             bands_g[v, block + z * HALO : block + (z + 1) * HALO, :] = band
-        return carry
-
-    lax.fori_loop(0, count, build, 0)
 
     def fill_side(v):
         for z in range(planes):
@@ -288,6 +289,7 @@
         blurred[v] = dot(bands_f[v], high) + dot(bands_f[v], low)
 
     for v in range(count):
+        build_rows(v)
         forward(v)
 
     for copy, side, dst in col_copies:
@@ -297,7 +299,6 @@
             take(*row_copy(v, j))
 
     def one_view(v):
-        fill_side(v)
         ox, oy = offs[v, 0, gx, gy], offs[v, 1, gx, gy]
         fx = subs[v, 0, gx, gy].astype(F32) * 0.25
         fy = subs[v, 1, gx, gy].astype(F32) * 0.25
@@ -311,19 +312,33 @@
         within = iota((1, EDGE, LANES), 1) + rest < EDGE
         deep = rows + EDGE
 
-        def plane(z):
-            here = ext[v, z, 0:deep, :]
+        def based(part):
+            here = part(0)
             for at in range(EDGE, 2 * HALO, EDGE):
-                here = jnp.where(oy + HALO >= at, ext[v, z, at : at + deep, :], here)
+                here = jnp.where(oy + HALO >= at, part(at), here)
             return here
 
+        strip_lane = iota((1, LANES), 1)
+
+        def mixed_strip(ref):
+            here = based(lambda at: ref[v, at : at + deep, :])
+            after = jnp.where(
+                strip_lane < (planes - 1) * HALO, pltpu.roll(here, LANES - HALO, 1), 0.0
+            )
+            return (1.0 - fz) * here + fz * after
+
+        left, right = mixed_strip(from_left), mixed_strip(from_right)
         below = None
         for z in range(planes - 1, -1, -1):
-            here = plane(z)
+            here = based(lambda at: ext[v, z, at : at + deep, 0:cols])
             flat = (1.0 - fz) * here
             if below is not None:
                 flat = flat + fz * below
             below = here
+            third = jnp.where(
+                strip_lane < LANES // 2, unpacked(right, z, True), unpacked(left, z, False)
+            )
+            flat = jnp.concatenate([flat, third], axis=1)
             flat = (1.0 - fx) * flat + fx * pltpu.roll(flat, wide - 1, 1)
             tiles = [
                 pltpu.roll(flat[:, c : c + LANES], shift, 1) for c in range(0, wide, LANES)
@@ -337,7 +352,10 @@
                 moved = jnp.where(within, moved[:-1], moved[1:]).reshape(rows, LANES)
                 at = pl.ds(z * rows, rows)
                 part = pl.ds(i * LANES, LANES)
-                ratio[v, at, part] = moved / blurred[v, at, part]
+                under = blurred[v, at, part]
+                inverse = pl.reciprocal(under, approx=True)
+                inverse = inverse * (2.0 - under * inverse)
+                ratio[v, at, part] = moved * inverse * (2.0 - under * inverse)
         high, low = split(ratio[v])
         spread = dot(bands_g[v], high) + dot(bands_g[v], low)
         high, low = split(spread)

time: 27.2 us -> 27.5 us (1.011)
  Pallas kernels: 25.1 us -> 25.4 us
where the time goes in v3:
time: 27.5 us; the launch traced here: 27.3 us
  Pallas kernels  25.4 us (92%)
  other arithmetic  1.9 us (7%)
    pallas_call x1, Pallas kernels, on_device(): pl.pallas_call(functools.partial(kernel, (count, planes, rows, cols)), ou...  25.4 us
    mul x1, other arithmetic, on_device(): return estimate * mean_back  1.9 us

profile of v3, /device:TPU:11, one launch (start us, length us, event | category | flops | bytes accessed | tf_op | source)
XLA Modules:
  0.0 27.3 jit_solution(12159047381933493077)
XLA Ops:
  0.0 0.0 copy-start
  0.0 25.4 %shard_map.73 = f32[8,64,256]{2,1,0:T(8,128)} custom-call(f32[8,64,256]{2,1,0:T(8,128)} %est.1, f32[4,8,64,256]{3,2,1,0:T(8,128)} %views.1, f32[4,15]{1,0:T(4,128)} %psf_x_in.1, f32[4,15]{1,0:T(4,128)} %psf_y_in.1, f32[4,15]{1,0:T(4,128)} %psf_z_in.1, s32[4,2,4,8]{3,2,1,0:T(4,128)} %bitcast.3, s32[4,3,4,8]{3,2,1,0:T(4,128)} %bitcast.2), custom_call_target="tpu_custom_call" | custom-call | tf_op jit(solution)/shard_map/pallas_call | solution.py:446
  25.4 0.0 copy-done
  25.4 1.9 %mul.3 = f32[8,64,256]{2,1,0:T(8,128)} multiply(f32[8,64,256]{2,1,0:T(8,128)S(1)} %copy-done, f32[8,64,256]{2,1,0:T(8,128)} %shard_map.73) | non-fusion elementwise | flops 131072 | bytes 1572864 | tf_op jit(solution)/shard_map/mul | solution.py:494
Async XLA Ops:
  0.0 25.4 %copy-start = (f32[8,64,256]{2,1,0:T(8,128)S(1)}, f32[8,64,256]{2,1,0:T(8,128)}, u32[]{:S(2)}) copy-start(f32[8,64,256]{2,1,0:T(8,128)} %est.1) | copy-start | bytes 1572868

commit v4 on v3

--- a/solution.py
+++ b/solution.py
@@ -169,24 +169,25 @@
         dst = ext.at[v, :, pl.ds(dst_at, dst_rows), pl.ds(0, cols)]
         return remote(src, dst, row_send.at[v, j], row_recv.at[v, j], side), side, dst
 
+    def col_copy(v, i):
+        side = COL_SIDES[i]
+        (src_at, src_rows), (dst_at, dst_rows) = rows_of(side[1], HALO)
+        own, land = (own_last, from_left) if side[0] == 1 else (own_first, from_right)
+        src = own.at[v, pl.ds(src_at, src_rows), :]
+        dst = land.at[v, pl.ds(dst_at, dst_rows), :]
+        return remote(src, dst, col_send.at[v, i], col_recv.at[v, i], side), side, dst
+
+    def copies_of(v):
+        found = [row_copy(v, j) for j in range(len(ROW_SIDES))]
+        return found + [col_copy(v, i) for i in range(len(COL_SIDES))]
+
     for v in range(count):
-        for j in range(2):
-            copy, side, _ = row_copy(v, j)
+        for copy, side, _ in copies_of(v)[: len(ROW_SIDES)]:
             if_there(side, copy.start)
-
-    for load in loads[:count]:
-        load.wait()
-    lax.fori_loop(0, count, lambda v, c: (strips(v), c)[1], 0)
-    col_copies = []
-    for i, side in enumerate(COL_SIDES):
-        dx, dy = side
-        (src_at, src_rows), (dst_at, dst_rows) = rows_of(dy, HALO)
-        own, land = (own_last, from_left) if dx == 1 else (own_first, from_right)
-        src = own.at[pl.ds(0, count), pl.ds(src_at, src_rows), :]
-        dst = land.at[pl.ds(0, count), pl.ds(dst_at, dst_rows), :]
-        copy = remote(src, dst, col_send.at[i], col_recv.at[i], side)
-        col_copies.append((copy, side, dst))
-        if_there(side, copy.start)
+        loads[v].wait()
+        strips(v)
+        for copy, side, _ in copies_of(v)[len(ROW_SIDES) :]:
+            if_there(side, copy.start)
 
     for load in small:
         load.wait()
@@ -292,13 +293,7 @@
         build_rows(v)
         forward(v)
 
-    for copy, side, dst in col_copies:
-        take(copy, side, dst)
-    for v in range(count):
-        for j in range(2):
-            take(*row_copy(v, j))
-
-    def one_view(v):
+    def warp(v):
         ox, oy = offs[v, 0, gx, gy], offs[v, 1, gx, gy]
         fx = subs[v, 0, gx, gy].astype(F32) * 0.25
         fy = subs[v, 1, gx, gy].astype(F32) * 0.25
@@ -356,6 +351,7 @@
                 inverse = pl.reciprocal(under, approx=True)
                 inverse = inverse * (2.0 - under * inverse)
                 ratio[v, at, part] = moved * inverse * (2.0 - under * inverse)
+    def spread_rows(v):
         high, low = split(ratio[v])
         spread = dot(bands_g[v], high) + dot(bands_g[v], low)
         high, low = split(spread)
@@ -364,7 +360,12 @@
         spread_low[:, at] = low
 
     for v in range(count):
-        one_view(v)
+        for copy, side, dst in copies_of(v):
+            take(copy, side, dst)
+        warp(v)
+        if v > 0:
+            spread_rows(v - 1)
+    spread_rows(count - 1)
 
     def along_cols(first, last, low, high):
         band = bands_t[:, :, low:high].reshape(count * cols, high - low)
@@ -401,11 +402,10 @@
 
     acc[...] = along_cols(0, block, 0, cols)
 
-    for copy, side, _ in est_copies + col_copies:
+    for copy, side, _ in est_copies:
         if_there(side, copy.wait_send)
     for v in range(count):
-        for j in range(2):
-            copy, side, _ = row_copy(v, j)
+        for copy, side, _ in copies_of(v):
             if_there(side, copy.wait_send)
     for copy, side, dst in end_copies:
         take(copy, side, dst)
@@ -482,8 +482,8 @@
             dma((len(SIDES),)),
             dma((count, 2)),
             dma((count, 2)),
-            dma((len(COL_SIDES),)),
-            dma((len(COL_SIDES),)),
+            dma((count, len(COL_SIDES))),
+            dma((count, len(COL_SIDES))),
             dma((len(SIDES),)),
             dma((len(SIDES),)),
         ],

time: 27.5 us -> 26.1 us (0.949)
  Pallas kernels: 25.4 us -> 24 us
    pallas_call x1, Pallas kernels: 25.4 us -> 24 us  [on_device(): pl.pallas_call(functools.partial(kernel, (count, planes, rows, cols)), ou...]
where the time goes in v4:
time: 26.1 us; the launch traced here: 25.9 us
  Pallas kernels  24 us (92%)
  other arithmetic  1.9 us (7%)
    pallas_call x1, Pallas kernels, on_device(): pl.pallas_call(functools.partial(kernel, (count, planes, rows, cols)), ou...  24 us
    mul x1, other arithmetic, on_device(): return estimate * mean_back  1.9 us

profile of v4, /device:TPU:11, one launch (start us, length us, event | category | flops | bytes accessed | tf_op | source)
XLA Modules:
  0.0 25.9 jit_solution(2392880990056818108)
XLA Ops:
  0.0 0.0 copy-start
  0.0 24.0 %shard_map.73 = f32[8,64,256]{2,1,0:T(8,128)} custom-call(f32[8,64,256]{2,1,0:T(8,128)} %est.1, f32[4,8,64,256]{3,2,1,0:T(8,128)} %views.1, f32[4,15]{1,0:T(4,128)} %psf_x_in.1, f32[4,15]{1,0:T(4,128)} %psf_y_in.1, f32[4,15]{1,0:T(4,128)} %psf_z_in.1, s32[4,2,4,8]{3,2,1,0:T(4,128)} %bitcast.3, s32[4,3,4,8]{3,2,1,0:T(4,128)} %bitcast.2), custom_call_target="tpu_custom_call" | custom-call | tf_op jit(solution)/shard_map/pallas_call | solution.py:446
  24.0 0.0 copy-done
  24.0 1.9 %mul.3 = f32[8,64,256]{2,1,0:T(8,128)} multiply(f32[8,64,256]{2,1,0:T(8,128)S(1)} %copy-done, f32[8,64,256]{2,1,0:T(8,128)} %shard_map.73) | non-fusion elementwise | flops 131072 | bytes 1572864 | tf_op jit(solution)/shard_map/mul | solution.py:494
Async XLA Ops:
  0.0 24.0 %copy-start = (f32[8,64,256]{2,1,0:T(8,128)S(1)}, f32[8,64,256]{2,1,0:T(8,128)}, u32[]{:S(2)}) copy-start(f32[8,64,256]{2,1,0:T(8,128)} %est.1) | copy-start | bytes 1572868

commit v5 on v4

--- a/solution.py
+++ b/solution.py
@@ -17,7 +17,6 @@
 
 SIDES = [(dx, dy) for dx in (-1, 0, 1) for dy in (-1, 0, 1) if (dx, dy) != (0, 0)]
 ROW_SIDES = [(0, -1), (0, 1)]
-COL_SIDES = [side for side in SIDES if side[0] != 0]
 
 
 def split(value):
@@ -170,23 +169,33 @@
         return remote(src, dst, row_send.at[v, j], row_recv.at[v, j], side), side, dst
 
     def col_copy(v, i):
-        side = COL_SIDES[i]
+        side = (2 * i - 1, 0)
+        own, land = (own_last, from_left) if i == 1 else (own_first, from_right)
+        dst = land.at[v, pl.ds(HALO, rows), :]
+        return remote(own.at[v], dst, col_send.at[v, i], col_recv.at[v, i], side), side, dst
+
+    def corner_copy(v, i, j):
+        side = ROW_SIDES[j]
+        land = (from_right, from_left)[i]
         (src_at, src_rows), (dst_at, dst_rows) = rows_of(side[1], HALO)
-        own, land = (own_last, from_left) if side[0] == 1 else (own_first, from_right)
-        src = own.at[v, pl.ds(src_at, src_rows), :]
+        src = land.at[v, pl.ds(HALO + src_at, src_rows), :]
         dst = land.at[v, pl.ds(dst_at, dst_rows), :]
-        return remote(src, dst, col_send.at[v, i], col_recv.at[v, i], side), side, dst
-
-    def copies_of(v):
-        found = [row_copy(v, j) for j in range(len(ROW_SIDES))]
-        return found + [col_copy(v, i) for i in range(len(COL_SIDES))]
+        k = 2 + 2 * i + j
+        return remote(src, dst, col_send.at[v, k], col_recv.at[v, k], side), side, dst
+
+    def rows_for(v):
+        return [row_copy(v, j) for j in range(2)]
+
+    def cols_for(v):
+        return [col_copy(v, i) for i in range(2)]
+
+    def corners_for(v):
+        return [corner_copy(v, i, j) for i in range(2) for j in range(2)]
 
     for v in range(count):
-        for copy, side, _ in copies_of(v)[: len(ROW_SIDES)]:
-            if_there(side, copy.start)
         loads[v].wait()
         strips(v)
-        for copy, side, _ in copies_of(v)[len(ROW_SIDES) :]:
+        for copy, side, _ in cols_for(v) + rows_for(v):
             if_there(side, copy.start)
 
     for load in small:
@@ -289,9 +298,15 @@
         high, low = split(along)
         blurred[v] = dot(bands_f[v], high) + dot(bands_f[v], low)
 
+    build_rows(0)
     for v in range(count):
-        build_rows(v)
         forward(v)
+        if v + 1 < count:
+            build_rows(v + 1)
+        for copy, side, dst in cols_for(v):
+            take(copy, side, dst)
+        for copy, side, _ in corners_for(v):
+            if_there(side, copy.start)
 
     def warp(v):
         ox, oy = offs[v, 0, gx, gy], offs[v, 1, gx, gy]
@@ -360,7 +375,7 @@
         spread_low[:, at] = low
 
     for v in range(count):
-        for copy, side, dst in copies_of(v):
+        for copy, side, dst in rows_for(v) + corners_for(v):
             take(copy, side, dst)
         warp(v)
         if v > 0:
@@ -405,7 +420,7 @@
     for copy, side, _ in est_copies:
         if_there(side, copy.wait_send)
     for v in range(count):
-        for copy, side, _ in copies_of(v):
+        for copy, side, _ in rows_for(v) + cols_for(v) + corners_for(v):
             if_there(side, copy.wait_send)
     for copy, side, dst in end_copies:
         take(copy, side, dst)
@@ -482,8 +497,8 @@
             dma((len(SIDES),)),
             dma((count, 2)),
             dma((count, 2)),
-            dma((count, len(COL_SIDES))),
-            dma((count, len(COL_SIDES))),
+            dma((count, 6)),
+            dma((count, 6)),
             dma((len(SIDES),)),
             dma((len(SIDES),)),
         ],

time: 26.1 us -> 28.7 us (1.100)
  Pallas kernels: 24 us -> 26.7 us
    pallas_call x1, Pallas kernels: 24 us -> 26.7 us  [on_device(): pl.pallas_call(functools.partial(kernel, (count, planes, rows, cols)), ou...]
where the time goes in v5:
time: 28.7 us; the launch traced here: 28.6 us
  Pallas kernels  26.7 us (93%)
  other arithmetic  1.9 us (7%)
    pallas_call x1, Pallas kernels, on_device(): pl.pallas_call(functools.partial(kernel, (count, planes, rows, cols)), ou...  26.7 us
    mul x1, other arithmetic, on_device(): return estimate * mean_back  1.9 us

profile of v5, /device:TPU:11, one launch (start us, length us, event | category | flops | bytes accessed | tf_op | source)
XLA Modules:
  0.0 28.6 jit_solution(1728319110342108454)
XLA Ops:
  0.0 0.0 copy-start
  0.0 26.7 %shard_map.73 = f32[8,64,256]{2,1,0:T(8,128)} custom-call(f32[8,64,256]{2,1,0:T(8,128)} %est.1, f32[4,8,64,256]{3,2,1,0:T(8,128)} %views.1, f32[4,15]{1,0:T(4,128)} %psf_x_in.1, f32[4,15]{1,0:T(4,128)} %psf_y_in.1, f32[4,15]{1,0:T(4,128)} %psf_z_in.1, s32[4,2,4,8]{3,2,1,0:T(4,128)} %bitcast.3, s32[4,3,4,8]{3,2,1,0:T(4,128)} %bitcast.2), custom_call_target="tpu_custom_call" | custom-call | tf_op jit(solution)/shard_map/pallas_call | solution.py:461
  26.7 0.0 copy-done
  26.7 1.9 %mul.3 = f32[8,64,256]{2,1,0:T(8,128)} multiply(f32[8,64,256]{2,1,0:T(8,128)S(1)} %copy-done, f32[8,64,256]{2,1,0:T(8,128)} %shard_map.73) | non-fusion elementwise | flops 131072 | bytes 1572864 | tf_op jit(solution)/shard_map/mul | solution.py:509
Async XLA Ops:
  0.0 26.7 %copy-start = (f32[8,64,256]{2,1,0:T(8,128)S(1)}, f32[8,64,256]{2,1,0:T(8,128)}, u32[]{:S(2)}) copy-start(f32[8,64,256]{2,1,0:T(8,128)} %est.1) | copy-start | bytes 1572868
